TPU v7x, 256 devices: a whole 4x4x8 slice. The times are simulated.
256 devices in a mesh: outer: 4 (over y_lo, core), atoms: 64 (over z, x, y_hi).
Axes of the slice: x: 4, y: 4 (y_hi: 2, y_lo: 2; y = y_hi * 2 + y_lo), z: 8, core: 2. Of those that a mesh axis runs over, the one named last changes fastest.
Arguments:
- features: float32 [262144, 128], P(('outer', 'atoms')), may hold values from -6 to 6
- positions: int32 [3, 262144], P(None, ('outer', 'atoms')), may hold values from 0 to 262143
- wavevectors: int32 [3, 768], replicated, may hold values from -6 to 6
- w_value: float32 [2, 128, 128], replicated, may hold values from -0.5 to 0.5
- freq_filter: float32 [2, 768, 128], replicated, may hold values from 0.05 to 1
- norm_gain: float32 [2, 128], replicated, may hold values from 0.1 to 1.9
- w_hidden: float32 [2, 128, 128], replicated, may hold values from -0.5 to 0.5
- b_hidden: float32 [2, 128], replicated, may hold values from -4 to 4
- w_output: float32 [2, 128, 128], replicated, may hold values from -0.5 to 0.5
Outputs:
- updated: float32 [262144, 128], P(('outer', 'atoms'))
All inputs are finite; a program needn't handle non-finite values.
Results may differ from a plain program's by a relative error of at most 0.0003.
Values sent between devices are 32-bit elements; how exact they have to be, the bound alone decides.
A program may use at most 64 MiB of HBM per device.

v0:
```python
import math

import jax
import jax.numpy as jnp
from jax import lax
from jax.sharding import PartitionSpec as P

fixed_scale = 262144
highest = lax.Precision.HIGHEST


def phases(pos_block, wave_block):
    integer_dot = pos_block[0][:, None] * wave_block[0][None, :]
    integer_dot = integer_dot + pos_block[1][:, None] * wave_block[1][None, :]
    integer_dot = integer_dot + pos_block[2][:, None] * wave_block[2][None, :]
    wrapped = jnp.mod(integer_dot, fixed_scale)
    return wrapped.astype(jnp.float32) * (2.0 * math.pi / fixed_scale)


def local(
    features, positions, wavevectors, w_value, freq_filter, norm_gain, w_hidden, b_hidden, w_output
):
    wave_count = wavevectors.shape[1]
    channel_count = features.shape[1]
    block_rows = min(256, wave_count)
    cos_parts = []
    sin_parts = []
    for offset in range(0, wave_count, block_rows):
        angles = phases(positions, wavevectors[:, offset : offset + block_rows])
        cos_parts.append(jnp.cos(angles))
        sin_parts.append(jnp.sin(angles))
    cos_table = jnp.concatenate(cos_parts, axis=1)
    sin_table = jnp.concatenate(sin_parts, axis=1)
    current = features
    for layer_index in range(w_value.shape[0]):
        projected = jnp.dot(
            current, w_value[layer_index], precision=highest, preferred_element_type=jnp.float32
        )
        real_part = jnp.einsum("ak,ac->kc", cos_table, projected, precision=highest)
        imag_part = -jnp.einsum("ak,ac->kc", sin_table, projected, precision=highest)
        factor = jnp.concatenate([real_part, imag_part], axis=1)
        filter_pair = jnp.concatenate([freq_filter[layer_index], freq_filter[layer_index]], axis=1)
        summed = lax.psum(factor, ("outer", "atoms"))
        filtered = summed * filter_pair
        messages = jnp.dot(
            cos_table,
            filtered[:, :channel_count],
            precision=highest,
            preferred_element_type=jnp.float32,
        )
        messages = messages - jnp.dot(
            sin_table,
            filtered[:, channel_count:],
            precision=highest,
            preferred_element_type=jnp.float32,
        )
        normed = (
            messages
            * lax.rsqrt(jnp.mean(messages * messages, axis=1, keepdims=True) + 1e-06)
            * norm_gain[layer_index]
        )
        hidden = jax.nn.silu(
            jnp.dot(
                normed, w_hidden[layer_index], precision=highest, preferred_element_type=jnp.float32
            )
            + b_hidden[layer_index]
        )
        current = current + jnp.dot(
            hidden, w_output[layer_index], precision=highest, preferred_element_type=jnp.float32
        )
    return current


def solution(mesh):
    placed = (
        P(("outer", "atoms"), None),
        P(None, ("outer", "atoms")),
        P(),
        P(),
        P(),
        P(),
        P(),
        P(),
        P(),
    )
    return jax.shard_map(
        local, mesh=mesh, in_specs=placed, out_specs=P(("outer", "atoms"), None), check_vma=False
    )
```

profile of v0, /device:TPU:1, one launch (start us, length us, event | category | flops | bytes accessed | tf_op | source)
XLA Modules:
  0.0 575.7 jit_solution(17106970901971007797)
XLA Ops:
  6.5 0.9 fusion.69
  7.4 0.8 fusion.68
  8.2 1.6 fusion.49
  9.9 13.1 %fusion.28 = (f32[1024,256]{1,0:T(8,128)S(1)}, f32[1024,256]{1,0:T(8,128)S(1)}, f32[1024,256]{1,0:T(8,128)S(1)}, f32[1024,256]{1,0:T(8,128)S(1)}, f32[1024,256]{1,0:T(8,128)S(1)}, /*index=5*/f32[1024,256]{1,0:T(8,128)S(1)}) fusion(s32[256]{0:T(256)S(1)} %bitcast.56, s32[1024]{0:T(1024)S(1)} %bitcast.49, s32[256]{0:T(256)S(1)} %bitcast.57, ...), kind=kLoop, calls=%fused_computation.53 | loop fusion | flops 14155776 | bytes 6312960 | tf_op jit(solution)/shard_map/cos | solution.py:30
  23.0 2.2 fusion.36
  25.2 2.2 convolution_negate_fusion.1
  27.4 1.0 pad_maximum_fusion.2
  28.6 1.2 fusion.67
  30.0 255.2 %all-reduce.3.cloned.1.call-done = f32[768,256]{0,1:T(8,128)} async-done(((f32[768,256]{0,1:T(8,128)}), f32[768,256]{0,1:T(8,128)}) %all-reduce.3.cloned.1.call-update) | async-done | bytes 786448 | tf_op jit(solution)/shard_map/psum | solution.py:43
  285.2 1.3 maximum_multiply_fusion
  286.6 5.0 fusion.33
  291.7 3.4 multiply_reduce_fusion.1
  295.1 1.1 convolution_add_fusion.3
  296.2 0.7 convolution_add_fusion.2
  297.1 0.6 fusion.45
  297.7 2.2 convolution_negate_fusion
  299.9 2.2 fusion.35
  302.1 1.2 pad_maximum_fusion.3
  303.5 253.0 %all-reduce.5.cloned.1.call-done = f32[768,256]{0,1:T(8,128)} async-done(((f32[768,256]{0,1:T(8,128)}), f32[768,256]{0,1:T(8,128)}) %all-reduce.5.cloned.1.call-update) | async-done | bytes 786448 | tf_op jit(solution)/shard_map/psum | solution.py:43
  556.4 1.3 maximum_multiply_fusion.1
  557.9 5.0 fusion.30
  562.9 3.4 multiply_reduce_fusion
  566.3 1.1 convolution_add_fusion.1
  567.4 1.4 convolution_add_fusion
  (43 shorter events, 1.2 us)
Async XLA Ops:
  6.5 278.6 %all-reduce.3.cloned.1.call-start = ((), (), s32[]{:S(2)}) async-start(), calls=%async_computation | async-start | bytes 1572864 | tf_op jit(solution)/shard_map/psum | solution.py:43
  23.0 2.2 copy-start.3
  23.0 2.2 copy-start.6
  23.0 2.2 copy-start.8
  23.0 2.2 copy-start
  28.4 1.6 copy-start.13
  28.4 1.6 copy-start.14
  28.4 528.0 %all-reduce.5.cloned.1.call-start = ((), (), s32[]{:S(2)}) async-start(), calls=%async_computation.1 | async-start | bytes 1572864 | tf_op jit(solution)/shard_map/psum | solution.py:43
  285.2 1.5 copy-start.4
  286.6 5.0 copy-start.1
  291.6 3.5 copy-start.12
  295.1 1.1 copy-start.10
  295.1 1.1 copy-start.15
  296.2 0.9 copy-start.11
  297.7 2.2 copy-start.7
  297.7 2.2 copy-start.9
  556.4 1.5 copy-start.5
  557.9 5.0 copy-start.2
  566.3 1.1 copy-start.16
Sparse Core Ops, SparseCore 0:
  28.5 256.6 all-reduce.2
  303.4 252.9 all-reduce.4
where the time goes:
time: 577 us; the launch traced here: 576 us
  waiting for transfers between devices  508 us (88%)
  matrix products  31.9 us (6%)
  other arithmetic  17.8 us (3%)
  between operations  13.8 us (2%)
    psum x2, waiting for transfers between devices, local(): summed = lax.psum(factor, ('outer', 'atoms'))  508 us
    cos x1, other arithmetic, local(): cos_parts.append(jnp.cos(angles))  13.1 us
  transfers between devices with their start and end apart: 2, of which 2 were waited for; matrix products, arithmetic and copies ran while one was open for 0% of the time, Pallas kernels for 0%

commit v1 on v0

v1 whole, which is shorter than its diff:
```python
import functools

import jax
import jax.numpy as jnp
from jax import lax
from jax.experimental import pallas as pl
from jax.experimental.pallas import tpu as pltpu
from jax.sharding import PartitionSpec as P

MESH = pl.DeviceIdType.MESH
f32 = jnp.float32
bf16 = jnp.bfloat16

NX, NY, NZ = 4, 4, 8
PLANE = NX * NY
ATOMS, CHANNELS, WAVES, BLOCKS = 1024, 128, 768, 2
ROWS = 2 * WAVES
HALF = ROWS // 2
CHUNKS = 3
CHUNK = HALF // CHUNKS
PIECE = CHUNK // PLANE
TURN = 262144.0

SIN = (
    6.283182818555351, -41.341421399021826, 81.59618388022938,
    -76.58010058938454, 41.20539511033188, -12.271262697277013,
)
COS = (
    0.999999989172279, -19.73920453209469, 64.93911898390982, -85.45016555036607,
    60.16783173144847, -25.968313301691698, 6.529610414314128,
)


def horner(coefficients, u):
    total = jnp.full_like(u, coefficients[-1])
    for c in coefficients[-2::-1]:
        total = total * u + c
    return total


def split(value):
    high = value.astype(bf16)
    return high, (value - high.astype(f32)).astype(bf16)


def dot(a, b):
    return jnp.dot(a, b, preferred_element_type=f32)


def dot_nt(a, b):
    return lax.dot_general(a, b, (((1,), (1,)), ((), ())), preferred_element_type=f32)


def hops(delta, size):
    return min(delta, size - delta)


PLANE_PEERS = sorted(
    ((dx, dy) for dx in range(NX) for dy in range(NY) if dx or dy),
    key=lambda d: -(hops(d[0], NX) + hops(d[1], NY)),
)
Z_PEERS = sorted(range(1, NZ), key=lambda d: -hops(d, NZ))


def body(
    feat_ref, pos_ref, wave_ref, wv_ref, filt_ref, gain_ref, wh_ref, bh_ref, wo_ref,
    out_ref,
    xs_ref, ws_ref, turn_ref, high_ref, low_ref, cur_ref, proj_ref, wvt_ref, wht_ref, wot_ref, bht_ref,
    away_ref, home_ref, cross_ref, plane_ref, mine_ref, depth_ref, fact_ref, acc_ref,
    cross_send, cross_recv, plane_send, plane_recv, depth_send, depth_recv,
    spread_send, spread_recv, pair_send, pair_recv,
    *, comm,
):
    outer, atoms = lax.axis_index("outer"), lax.axis_index("atoms")
    core, y = outer % 2, (atoms % 2) * 2 + outer // 2
    x, z = (atoms // 2) % NX, atoms // (2 * NX)
    me = x * NY + y

    def device(x, y, z, core):
        return ((y % 2) * 2 + core, z * (2 * NX) + x * 2 + y // 2)

    def plane_peer(delta):
        px, py = (x + delta[0]) % NX, (y + delta[1]) % NY
        return px * NY + py, device(px, py, z, core)

    other_core = device(x, y, z, 1 - core)

    def z_peer(delta):
        return device(x, y, (z + delta) % NZ, core)

    def send(source, target, send_sem, recv_sem, to):
        if comm:
            pltpu.make_async_remote_copy(
                src_ref=source, dst_ref=target, send_sem=send_sem, recv_sem=recv_sem,
                device_id=to, device_id_type=MESH,
            ).start()

    def wait(like, sem):
        if comm:
            pltpu.make_async_copy(like, like, sem).wait()

    if comm:
        barrier = pltpu.get_barrier_semaphore()
        for delta in PLANE_PEERS:
            pl.semaphore_signal(barrier, 1, device_id=plane_peer(delta)[1], device_id_type=MESH)
        for delta in Z_PEERS:
            pl.semaphore_signal(barrier, 1, device_id=z_peer(delta), device_id_type=MESH)
        pl.semaphore_signal(barrier, 1, device_id=other_core, device_id_type=MESH)

    positions = pos_ref[...]
    waves = wave_ref[...].astype(f32)
    xs_ref[...] = jnp.zeros_like(xs_ref)
    ws_ref[...] = jnp.zeros_like(ws_ref)
    for i in range(3):
        xs_ref[3 * i : 3 * i + 3, :] = ((positions >> (8 * i)) & 255).astype(f32)
        ws_ref[3 * i : 3 * i + 3, :] = waves * (256.0**i / TURN)
    turn_ref[...] = dot(ws_ref[...].T.astype(bf16), xs_ref[...].astype(bf16))

    for b in range(BLOCKS):
        for matrix, held in ((wv_ref[b], wvt_ref), (wh_ref[b] * gain_ref[b : b + 1, :].T, wht_ref), (wo_ref[b], wot_ref)):
            high, low = split(matrix.T)
            held[b, :CHANNELS, :] = high
            held[b, CHANNELS:, :] = low
        bht_ref[b] = jnp.broadcast_to(bh_ref[b : b + 1, :], (CHANNELS, CHANNELS)).T
    cur_ref[...] = feat_ref[...].T

    def weighted(held, b, value):
        high, low = split(value)
        both = dot(held[b], high)
        return both[:CHANNELS] + both[CHANNELS:] + dot(held[b, :CHANNELS, :], low)

    def project(b):
        high, low = split(weighted(wvt_ref, b, cur_ref[...]))
        proj_ref[:CHANNELS, :] = high
        proj_ref[CHANNELS:, :] = low

    def table(first_octet, count):
        def step(i, _):
            octet = first_octet + i
            t = turn_ref[pl.ds(pl.multiple_of(octet * 8, 8), 8), :]
            r = t - jnp.round(t)
            u = r * r
            pair = jnp.concatenate([horner(COS, u), horner(SIN, u) * r], axis=0)
            high, low = split(pair)
            at = pl.ds(pl.multiple_of(octet * 16, 16), 16)
            high_ref[at, :] = high
            low_ref[at, :] = low
            return 0

        lax.fori_loop(0, count, step, 0)

    project(0)
    for b in range(BLOCKS):
        for which in range(2):
            half = 1 - core if which == 0 else core
            for q in range(CHUNKS):
                chunk = half * CHUNKS + q
                if b == 0:
                    table(chunk * (CHUNK // 16), CHUNK // 16)
                rows = pl.ds(pl.multiple_of(chunk * CHUNK, CHUNK), CHUNK)
                both = dot_nt(high_ref[rows, :], proj_ref[...]) + dot_nt(low_ref[rows, :], proj_ref[...])
                part = both[:, :CHANNELS] + both[:, CHANNELS:]
                if which == 0:
                    away_ref[b, q] = part
                    if comm and b == 0 and q == 0:
                        pl.semaphore_wait(barrier, len(PLANE_PEERS) + len(Z_PEERS) + 1)
                    send(away_ref.at[b, q], cross_ref.at[b, q], cross_send.at[b, q], cross_recv.at[b, q], other_core)
                else:
                    wait(cross_ref.at[b, q], cross_recv.at[b, q])
                    home_ref[b, q] = part + cross_ref[b, q]
                    for delta in PLANE_PEERS:
                        peer, to = plane_peer(delta)
                        send(
                            home_ref.at[b, q, pl.ds(pl.multiple_of(peer * PIECE, 8), PIECE)],
                            plane_ref.at[b, q, me], plane_send.at[b, q], plane_recv.at[b, q], to,
                        )
                    plane_ref[b, q, me] = home_ref[b, q, pl.ds(pl.multiple_of(me * PIECE, 8), PIECE)]
        for q in range(CHUNKS):
            wait(plane_ref.at[b, q, pl.ds(0, PLANE - 1)], plane_recv.at[b, q])
            mine_ref[b, q] = jnp.sum(plane_ref[b, q], axis=0)
            for delta in Z_PEERS:
                send(mine_ref.at[b, q], depth_ref.at[b, q, z], depth_send.at[b, q], depth_recv.at[b, q], z_peer(delta))
            depth_ref[b, q, z] = mine_ref[b, q]
        for q in range(CHUNKS):
            wait(depth_ref.at[b, q, pl.ds(0, NZ - 1)], depth_recv.at[b, q])
            total = jnp.sum(depth_ref[b, q], axis=0)
            first = (core * CHUNKS + q) * CHUNK + me * PIECE
            parts = []
            for i in range(PIECE // 8):
                octet = (first // 8 + i) // 2
                parts.append(filt_ref[b, pl.ds(pl.multiple_of(octet * 8, 8), 8), :])
            here = fact_ref.at[b, pl.ds(pl.multiple_of(first, 8), PIECE)]
            here[...] = total * jnp.concatenate(parts, axis=0)
            for delta in PLANE_PEERS:
                send(here, here, spread_send.at[b, q], spread_recv.at[b, q], plane_peer(delta)[1])
        for q in range(CHUNKS):
            chunk = pl.ds(pl.multiple_of((core * CHUNKS + q) * CHUNK, CHUNK), CHUNK)
            wait(fact_ref.at[b, pl.ds(0, (PLANE - 1) * PIECE)], spread_recv.at[b, q])
            whole = fact_ref.at[b, chunk]
            send(whole, whole, pair_send.at[b, q], pair_recv.at[b, q], other_core)
        for which in range(2):
            half = core if which == 0 else 1 - core
            if which == 1:
                for q in range(CHUNKS):
                    wait(fact_ref.at[b, pl.ds(0, CHUNK)], pair_recv.at[b, q])
            rows = pl.ds(pl.multiple_of(half * HALF, HALF), HALF)
            high, low = split(fact_ref[b, rows, :].T)
            both = dot(jnp.concatenate([high, low], axis=0), high_ref[rows, :])
            part = both[:CHANNELS] + both[CHANNELS:] + dot(high, low_ref[rows, :])
            if which == 0:
                acc_ref[...] = part
            else:
                acc_ref[...] += part
        messages = acc_ref[...]
        scale = lax.rsqrt(jnp.mean(messages * messages, axis=0, keepdims=True) + 1e-6)
        bias = jnp.concatenate([bht_ref[b]] * (ATOMS // CHANNELS), axis=1)
        v = weighted(wht_ref, b, messages) * scale + bias
        hidden = v / (1.0 + jnp.exp(-v))
        cur_ref[...] += weighted(wot_ref, b, hidden)
        if b + 1 < BLOCKS:
            project(b + 1)
    out_ref[...] = cur_ref[...].T
    for b in range(BLOCKS):
        for q in range(CHUNKS):
            wait(away_ref.at[b, q], cross_send.at[b, q])
            wait(plane_ref.at[b, q, pl.ds(0, PLANE - 1)], plane_send.at[b, q])
            wait(depth_ref.at[b, q, pl.ds(0, NZ - 1)], depth_send.at[b, q])
            wait(fact_ref.at[b, pl.ds(0, (PLANE - 1) * PIECE)], spread_send.at[b, q])
            wait(fact_ref.at[b, pl.ds(0, CHUNK)], pair_send.at[b, q])


def local(*operands, comm=True):
    sems = [pltpu.SemaphoreType.DMA((BLOCKS, CHUNKS))] * 10
    return pl.pallas_call(
        functools.partial(body, comm=comm),
        name="ewald",
        out_shape=jax.ShapeDtypeStruct((ATOMS, CHANNELS), f32),
        in_specs=[pl.BlockSpec(memory_space=pltpu.VMEM)] * len(operands),
        out_specs=pl.BlockSpec(memory_space=pltpu.VMEM),
        scratch_shapes=[
            pltpu.VMEM((16, ATOMS), f32),
            pltpu.VMEM((16, WAVES), f32),
            pltpu.VMEM((WAVES, ATOMS), f32),
            pltpu.VMEM((ROWS, ATOMS), bf16),
            pltpu.VMEM((ROWS, ATOMS), bf16),
            pltpu.VMEM((CHANNELS, ATOMS), f32),
            pltpu.VMEM((2 * CHANNELS, ATOMS), bf16),
            pltpu.VMEM((BLOCKS, 2 * CHANNELS, CHANNELS), bf16),
            pltpu.VMEM((BLOCKS, 2 * CHANNELS, CHANNELS), bf16),
            pltpu.VMEM((BLOCKS, 2 * CHANNELS, CHANNELS), bf16),
            pltpu.VMEM((BLOCKS, CHANNELS, CHANNELS), f32),
            pltpu.VMEM((BLOCKS, CHUNKS, CHUNK, CHANNELS), f32),
            pltpu.VMEM((BLOCKS, CHUNKS, CHUNK, CHANNELS), f32),
            pltpu.VMEM((BLOCKS, CHUNKS, CHUNK, CHANNELS), f32),
            pltpu.VMEM((BLOCKS, CHUNKS, PLANE, PIECE, CHANNELS), f32),
            pltpu.VMEM((BLOCKS, CHUNKS, PIECE, CHANNELS), f32),
            pltpu.VMEM((BLOCKS, CHUNKS, NZ, PIECE, CHANNELS), f32),
            pltpu.VMEM((BLOCKS, ROWS, CHANNELS), f32),
            pltpu.VMEM((CHANNELS, ATOMS), f32),
            *sems,
        ],
        compiler_params=pltpu.CompilerParams(
            collective_id=0 if comm else None,
            has_side_effects=True,
            vmem_limit_bytes=56 << 20,
        ),
    )(*operands)


def solution(mesh):
    rows = P(("outer", "atoms"), None)
    return jax.shard_map(
        local,
        mesh=mesh,
        in_specs=(rows, P(None, ("outer", "atoms")), *[P()] * 7),
        out_specs=rows,
        check_vma=False,
    )
```

time: 577 us -> 62.4 us (0.11)
  waiting for transfers between devices: 508 us -> 0 us
  Pallas kernels: 0 us -> 60.3 us
  matrix products: 31.9 us -> 0 us
  other arithmetic: 17.8 us -> 0 us
  between operations: 13.8 us -> 0.01 us
    psum x2 -> x0, waiting for transfers between devices: 508 us -> none  [local(): summed = lax.psum(factor, ('outer', 'atoms'))]
    pallas_call x0 -> x1, Pallas kernels: none -> 60.3 us  [local(): pl.pallas_call(functools.partial(body, comm=comm), name='ewald', out_shap...]
    dot_general x14 -> x0, matrix products: 31.9 us -> none  [the longest x2 9.98 us: local(): jnp.dot(cos_table, filtered[:, :channel_count], precision=highest, prefer...]
    cos x1 -> x0, other arithmetic: 13.1 us -> none  [local(): cos_parts.append(jnp.cos(angles))]
  transfers between devices with their start and end apart: 2 -> 0, of which waited for: 2 -> 0; matrix products, arithmetic and copies ran while one was open for 0% -> 0% of each run, Pallas kernels for 0% -> 0%
where the time goes in v1:
time: 62.4 us; the launch traced here: 62.2 us
  Pallas kernels  60.3 us (97%)
  local copies, waits for them, and re-layouts  1.87 us (3%)
    pallas_call x1, Pallas kernels, local(): pl.pallas_call(functools.partial(body, comm=comm), name='ewald', out_shap...  60.3 us
    unnamed x1, local copies, waits for them, and re-layouts  1.87 us

profile of v1, /device:TPU:1, one launch (start us, length us, event | category | flops | bytes accessed | tf_op | source)
XLA Modules:
  0.0 62.2 jit_solution(841245352329829874)
XLA Ops:
  0.0 60.3 %ewald.1 = f32[1024,128]{1,0:T(8,128)} custom-call(f32[1024,128]{1,0:T(8,128)} %feat_ref.1, s32[3,1024]{1,0:T(4,128)} %pos_ref.1, s32[3,768]{1,0:T(4,128)} %wave_ref.1, f32[2,128,128]{2,1,0:T(8,128)} %wv_ref.1, f32[2,768,128]{2,1,0:T(8,128)} %filt_ref.1, f32[2,128]{1,0:T(2,128)} %gain_ref.1, f32[2,128,128]{2,1,0:T(8,128)} %wh_ref.1, f32[2,128]{1,0:T(2,128)} %bh_ref.1, ...), custom_call_target="tpu_custom_call" | custom-call | tf_op jit(solution)/shard_map/ewald/pallas_call | solution.py:234
  60.4 1.9 %copy.11 = f32[1024,128]{1,0:T(8,128)} copy(f32[1024,128]{1,0:T(8,128)} %ewald.1) | data formatting | bytes 1048576

commit v2 on v1

--- a/solution.py
+++ b/solution.py
@@ -20,15 +20,11 @@
 CHUNK = HALF // CHUNKS
 PIECE = CHUNK // PLANE
 TURN = 262144.0
-
-SIN = (
-    6.283182818555351, -41.341421399021826, 81.59618388022938,
-    -76.58010058938454, 41.20539511033188, -12.271262697277013,
-)
-COS = (
-    0.999999989172279, -19.73920453209469, 64.93911898390982, -85.45016555036607,
-    60.16783173144847, -25.968313301691698, 6.529610414314128,
-)
+GROUP = 32
+TAIL = ((0, CHUNKS - 1), (CHUNKS - 1, CHUNKS))
+
+SIN = (4.442882834149947, -7.308241154547219, 3.6062889582380353, -0.8457635962127477, 0.10920575375428615)
+COS = (1.4142134965650266, -6.978850988240709, 5.739461170716688, -1.8835629875263915, 0.31069819226115863)
 
 
 def horner(coefficients, u):
@@ -63,14 +59,28 @@
 
 
 def body(
+    feat_hbm, pos_hbm, wave_hbm, wv_hbm, filt_hbm, gain_hbm, wh_hbm, bh_hbm, wo_hbm,
+    out_ref,
     feat_ref, pos_ref, wave_ref, wv_ref, filt_ref, gain_ref, wh_ref, bh_ref, wo_ref,
-    out_ref,
     xs_ref, ws_ref, turn_ref, high_ref, low_ref, cur_ref, proj_ref, wvt_ref, wht_ref, wot_ref, bht_ref,
     away_ref, home_ref, cross_ref, plane_ref, mine_ref, depth_ref, fact_ref, acc_ref,
+    load_sem,
     cross_send, cross_recv, plane_send, plane_recv, depth_send, depth_recv,
     spread_send, spread_recv, pair_send, pair_recv,
     *, comm,
 ):
+    loads = [
+        pltpu.make_async_copy(source, target, load_sem.at[i])
+        for i, (source, target) in enumerate(
+            (
+                (pos_hbm, pos_ref), (wave_hbm, wave_ref), (feat_hbm, feat_ref), (wv_hbm, wv_ref), (gain_hbm, gain_ref),
+                (wh_hbm, wh_ref), (bh_hbm, bh_ref), (wo_hbm, wo_ref), (filt_hbm, filt_ref),
+            )
+        )
+    ]
+    for copy in loads:
+        copy.start()
+
     outer, atoms = lax.axis_index("outer"), lax.axis_index("atoms")
     core, y = outer % 2, (atoms % 2) * 2 + outer // 2
     x, z = (atoms // 2) % NX, atoms // (2 * NX)
@@ -107,6 +117,8 @@
             pl.semaphore_signal(barrier, 1, device_id=z_peer(delta), device_id_type=MESH)
         pl.semaphore_signal(barrier, 1, device_id=other_core, device_id_type=MESH)
 
+    for copy in loads[:2]:
+        copy.wait()
     positions = pos_ref[...]
     waves = wave_ref[...].astype(f32)
     xs_ref[...] = jnp.zeros_like(xs_ref)
@@ -116,13 +128,10 @@
         ws_ref[3 * i : 3 * i + 3, :] = waves * (256.0**i / TURN)
     turn_ref[...] = dot(ws_ref[...].T.astype(bf16), xs_ref[...].astype(bf16))
 
-    for b in range(BLOCKS):
-        for matrix, held in ((wv_ref[b], wvt_ref), (wh_ref[b] * gain_ref[b : b + 1, :].T, wht_ref), (wo_ref[b], wot_ref)):
-            high, low = split(matrix.T)
-            held[b, :CHANNELS, :] = high
-            held[b, CHANNELS:, :] = low
-        bht_ref[b] = jnp.broadcast_to(bh_ref[b : b + 1, :], (CHANNELS, CHANNELS)).T
-    cur_ref[...] = feat_ref[...].T
+    def transposed(matrix, held, b):
+        high, low = split(matrix.T)
+        held[b, :CHANNELS, :] = high
+        held[b, CHANNELS:, :] = low
 
     def weighted(held, b, value):
         high, low = split(value)
@@ -130,51 +139,71 @@
         return both[:CHANNELS] + both[CHANNELS:] + dot(held[b, :CHANNELS, :], low)
 
     def project(b):
-        high, low = split(weighted(wvt_ref, b, cur_ref[...]))
-        proj_ref[:CHANNELS, :] = high
-        proj_ref[CHANNELS:, :] = low
-
-    def table(first_octet, count):
+        high, low = split(weighted(wvt_ref, b, cur_ref[...]).T)
+        proj_ref[:, :CHANNELS] = high
+        proj_ref[:, CHANNELS:] = low
+
+    def chunk_rows(chunk):
+        return pl.ds(pl.multiple_of(chunk * CHUNK, CHUNK), CHUNK)
+
+    def table(chunk):
         def step(i, _):
-            octet = first_octet + i
-            t = turn_ref[pl.ds(pl.multiple_of(octet * 8, 8), 8), :]
-            r = t - jnp.round(t)
-            u = r * r
-            pair = jnp.concatenate([horner(COS, u), horner(SIN, u) * r], axis=0)
-            high, low = split(pair)
-            at = pl.ds(pl.multiple_of(octet * 16, 16), 16)
-            high_ref[at, :] = high
-            low_ref[at, :] = low
+            for j in range(GROUP // 16):
+                octet = chunk * (CHUNK // 16) + i * (GROUP // 16) + j
+                t = turn_ref[pl.ds(pl.multiple_of(octet * 8, 8), 8), :]
+                r = t - jnp.round(t)
+                u = r * r
+                s = horner(SIN, u) * r
+                high, low = split(jnp.concatenate([1.0 - s * s, s * horner(COS, u)], axis=0))
+                at = pl.ds(pl.multiple_of(octet * 16, 16), 16)
+                high_ref[at, :] = high
+                low_ref[at, :] = low
             return 0
 
-        lax.fori_loop(0, count, step, 0)
-
+        lax.fori_loop(0, CHUNK // GROUP, step, 0)
+
+    def factor(rows):
+        a = dot(high_ref[rows, :], proj_ref[...])
+        b = dot(low_ref[rows, :], proj_ref[...])
+        return (a[:, :CHANNELS] + a[:, CHANNELS:]) + (b[:, :CHANNELS] + b[:, CHANNELS:])
+
+    for copy in loads[2:4]:
+        copy.wait()
+    for b in range(BLOCKS):
+        transposed(wv_ref[b], wvt_ref, b)
+    cur_ref[...] = feat_ref[...].T
     project(0)
     for b in range(BLOCKS):
-        for which in range(2):
-            half = 1 - core if which == 0 else core
-            for q in range(CHUNKS):
-                chunk = half * CHUNKS + q
-                if b == 0:
-                    table(chunk * (CHUNK // 16), CHUNK // 16)
-                rows = pl.ds(pl.multiple_of(chunk * CHUNK, CHUNK), CHUNK)
-                both = dot_nt(high_ref[rows, :], proj_ref[...]) + dot_nt(low_ref[rows, :], proj_ref[...])
-                part = both[:, :CHANNELS] + both[:, CHANNELS:]
-                if which == 0:
-                    away_ref[b, q] = part
-                    if comm and b == 0 and q == 0:
-                        pl.semaphore_wait(barrier, len(PLANE_PEERS) + len(Z_PEERS) + 1)
-                    send(away_ref.at[b, q], cross_ref.at[b, q], cross_send.at[b, q], cross_recv.at[b, q], other_core)
-                else:
-                    wait(cross_ref.at[b, q], cross_recv.at[b, q])
-                    home_ref[b, q] = part + cross_ref[b, q]
-                    for delta in PLANE_PEERS:
-                        peer, to = plane_peer(delta)
-                        send(
-                            home_ref.at[b, q, pl.ds(pl.multiple_of(peer * PIECE, 8), PIECE)],
-                            plane_ref.at[b, q, me], plane_send.at[b, q], plane_recv.at[b, q], to,
-                        )
-                    plane_ref[b, q, me] = home_ref[b, q, pl.ds(pl.multiple_of(me * PIECE, 8), PIECE)]
+        order = [(1 - core) * CHUNKS + q for q in range(CHUNKS)] + [core * CHUNKS + q for q in range(CHUNKS)]
+        if b == 0:
+            table(order[0])
+        for k, chunk in enumerate(order):
+            q = k % CHUNKS
+            part_ref = away_ref.at[b, q] if k < CHUNKS else home_ref.at[b, q]
+            part_ref[...] = factor(chunk_rows(chunk))
+            if b == 0 and k + 1 < len(order):
+                table(order[k + 1])
+            if k < CHUNKS:
+                if comm and b == 0 and q == 0:
+                    pl.semaphore_wait(barrier, len(PLANE_PEERS) + len(Z_PEERS) + 1)
+                send(part_ref, cross_ref.at[b, q], cross_send.at[b, q], cross_recv.at[b, q], other_core)
+            else:
+                wait(cross_ref.at[b, q], cross_recv.at[b, q])
+                part_ref[...] += cross_ref[b, q]
+                for delta in PLANE_PEERS:
+                    peer, to = plane_peer(delta)
+                    send(
+                        home_ref.at[b, q, pl.ds(pl.multiple_of(peer * PIECE, 8), PIECE)],
+                        plane_ref.at[b, q, me], plane_send.at[b, q], plane_recv.at[b, q], to,
+                    )
+                plane_ref[b, q, me] = home_ref[b, q, pl.ds(pl.multiple_of(me * PIECE, 8), PIECE)]
+        if b == 0:
+            for copy in loads[4:]:
+                copy.wait()
+            for i in range(BLOCKS):
+                transposed(wh_ref[i] * gain_ref[i : i + 1, :].T, wht_ref, i)
+                transposed(wo_ref[i], wot_ref, i)
+                bht_ref[i] = jnp.broadcast_to(bh_ref[i : i + 1, :], (CHANNELS, CHANNELS)).T
         for q in range(CHUNKS):
             wait(plane_ref.at[b, q, pl.ds(0, PLANE - 1)], plane_recv.at[b, q])
             mine_ref[b, q] = jnp.sum(plane_ref[b, q], axis=0)
@@ -198,19 +227,16 @@
             wait(fact_ref.at[b, pl.ds(0, (PLANE - 1) * PIECE)], spread_recv.at[b, q])
             whole = fact_ref.at[b, chunk]
             send(whole, whole, pair_send.at[b, q], pair_recv.at[b, q], other_core)
-        for which in range(2):
-            half = core if which == 0 else 1 - core
-            if which == 1:
-                for q in range(CHUNKS):
-                    wait(fact_ref.at[b, pl.ds(0, CHUNK)], pair_recv.at[b, q])
-            rows = pl.ds(pl.multiple_of(half * HALF, HALF), HALF)
+        def message(rows):
             high, low = split(fact_ref[b, rows, :].T)
             both = dot(jnp.concatenate([high, low], axis=0), high_ref[rows, :])
-            part = both[:CHANNELS] + both[CHANNELS:] + dot(high, low_ref[rows, :])
-            if which == 0:
-                acc_ref[...] = part
-            else:
-                acc_ref[...] += part
+            return both[:CHANNELS] + both[CHANNELS:] + dot(high, low_ref[rows, :])
+
+        acc_ref[...] = message(pl.ds(pl.multiple_of(core * HALF, HALF), HALF))
+        for first, last in TAIL:
+            for q in range(first, last):
+                wait(fact_ref.at[b, pl.ds(0, CHUNK)], pair_recv.at[b, q])
+            acc_ref[...] += message(pl.ds(pl.multiple_of((1 - core) * HALF + first * CHUNK, 128), (last - first) * CHUNK))
         messages = acc_ref[...]
         scale = lax.rsqrt(jnp.mean(messages * messages, axis=0, keepdims=True) + 1e-6)
         bias = jnp.concatenate([bht_ref[b]] * (ATOMS // CHANNELS), axis=1)
@@ -234,17 +260,18 @@
     return pl.pallas_call(
         functools.partial(body, comm=comm),
         name="ewald",
-        out_shape=jax.ShapeDtypeStruct((ATOMS, CHANNELS), f32),
-        in_specs=[pl.BlockSpec(memory_space=pltpu.VMEM)] * len(operands),
+        out_shape=pltpu.VMEM((ATOMS, CHANNELS), f32),
+        in_specs=[pl.BlockSpec(memory_space=pltpu.HBM)] * len(operands),
         out_specs=pl.BlockSpec(memory_space=pltpu.VMEM),
         scratch_shapes=[
+            *[pltpu.VMEM(operand.shape, operand.dtype) for operand in operands],
             pltpu.VMEM((16, ATOMS), f32),
             pltpu.VMEM((16, WAVES), f32),
             pltpu.VMEM((WAVES, ATOMS), f32),
             pltpu.VMEM((ROWS, ATOMS), bf16),
             pltpu.VMEM((ROWS, ATOMS), bf16),
             pltpu.VMEM((CHANNELS, ATOMS), f32),
-            pltpu.VMEM((2 * CHANNELS, ATOMS), bf16),
+            pltpu.VMEM((ATOMS, 2 * CHANNELS), bf16),
             pltpu.VMEM((BLOCKS, 2 * CHANNELS, CHANNELS), bf16),
             pltpu.VMEM((BLOCKS, 2 * CHANNELS, CHANNELS), bf16),
             pltpu.VMEM((BLOCKS, 2 * CHANNELS, CHANNELS), bf16),
@@ -257,6 +284,7 @@
             pltpu.VMEM((BLOCKS, CHUNKS, NZ, PIECE, CHANNELS), f32),
             pltpu.VMEM((BLOCKS, ROWS, CHANNELS), f32),
             pltpu.VMEM((CHANNELS, ATOMS), f32),
+            pltpu.SemaphoreType.DMA((9,)),
             *sems,
         ],
         compiler_params=pltpu.CompilerParams(

time: 62.4 us -> 56.5 us (0.905)
  Pallas kernels: 60.3 us -> 55.6 us
  local copies, waits for them, and re-layouts: 1.87 us -> 0.8 us
    pallas_call x1, Pallas kernels: 60.3 us -> 55.6 us  [local(): pl.pallas_call(functools.partial(body, comm=comm), name='ewald', out_shap...]
    unnamed x1, local copies, waits for them, and re-layouts: 1.87 us -> 0.8 us
where the time goes in v2:
time: 56.5 us; the launch traced here: 56.4 us
  Pallas kernels  55.6 us (98%)
  local copies, waits for them, and re-layouts  0.8 us (1%)
    pallas_call x1, Pallas kernels, local(): pl.pallas_call(functools.partial(body, comm=comm), name='ewald', out_shap...  55.6 us

profile of v2, /device:TPU:1, one launch (start us, length us, event | category | flops | bytes accessed | tf_op | source)
XLA Modules:
  0.0 56.4 jit_solution(3794438611558522588)
XLA Ops:
  0.0 55.6 %ewald.1 = f32[1024,128]{1,0:T(8,128)S(1)} custom-call(f32[1024,128]{1,0:T(8,128)} %feat_hbm.1, s32[3,1024]{1,0:T(4,128)} %pos_hbm.1, s32[3,768]{1,0:T(4,128)} %wave_hbm.1, f32[2,128,128]{2,1,0:T(8,128)} %wv_hbm.1, f32[2,768,128]{2,1,0:T(8,128)} %filt_hbm.1, f32[2,128]{1,0:T(2,128)} %gain_hbm.1, f32[2,128,128]{2,1,0:T(8,128)} %wh_hbm.1, f32[2,128]{1,0:T(2,128)} %bh_hbm.1, ...), custom_call_target="tpu_custom_call" | custom-call | tf_op jit(solution)/shard_map/ewald/pallas_call | solution.py:260
  55.6 0.8 %copy.11 = f32[1024,128]{1,0:T(8,128)} copy(f32[1024,128]{1,0:T(8,128)S(1)} %ewald.1) | data formatting | bytes 1048576

commit v3 on v2

--- a/solution.py
+++ b/solution.py
@@ -20,6 +20,7 @@
 CHUNK = HALF // CHUNKS
 PIECE = CHUNK // PLANE
 TURN = 262144.0
+FUSED = 256
 GROUP = 32
 TAIL = ((0, CHUNKS - 1), (CHUNKS - 1, CHUNKS))
 
@@ -147,9 +148,11 @@
         return pl.ds(pl.multiple_of(chunk * CHUNK, CHUNK), CHUNK)
 
     def table(chunk):
-        def step(i, _):
-            for j in range(GROUP // 16):
-                octet = chunk * (CHUNK // 16) + i * (GROUP // 16) + j
+        table_rows(chunk, 0, CHUNK)
+
+    def table_rows(chunk, i, group):
+            for j in range(group // 16):
+                octet = chunk * (CHUNK // 16) + i * (group // 16) + j
                 t = turn_ref[pl.ds(pl.multiple_of(octet * 8, 8), 8), :]
                 r = t - jnp.round(t)
                 u = r * r
@@ -158,49 +161,74 @@
                 at = pl.ds(pl.multiple_of(octet * 16, 16), 16)
                 high_ref[at, :] = high
                 low_ref[at, :] = low
-            return 0
-
-        lax.fori_loop(0, CHUNK // GROUP, step, 0)
 
     def factor(rows):
         a = dot(high_ref[rows, :], proj_ref[...])
-        b = dot(low_ref[rows, :], proj_ref[...])
-        return (a[:, :CHANNELS] + a[:, CHANNELS:]) + (b[:, :CHANNELS] + b[:, CHANNELS:])
-
+        b = dot(low_ref[rows, :], proj_ref[:, :CHANNELS])
+        return (a[:, :CHANNELS] + a[:, CHANNELS:]) + b
+
+    def hand_over(b, q):
+        send(away_ref.at[b, q], cross_ref.at[b, q], cross_send.at[b, q], cross_recv.at[b, q], other_core)
+
+    def reduce_plane(b, q):
+        wait(cross_ref.at[b, q], cross_recv.at[b, q])
+        home_ref[b, q] += cross_ref[b, q]
+        for delta in PLANE_PEERS:
+            peer, to = plane_peer(delta)
+            send(
+                home_ref.at[b, q, pl.ds(pl.multiple_of(peer * PIECE, 8), PIECE)],
+                plane_ref.at[b, q, me], plane_send.at[b, q], plane_recv.at[b, q], to,
+            )
+        plane_ref[b, q, me] = home_ref[b, q, pl.ds(pl.multiple_of(me * PIECE, 8), PIECE)]
+
+    table((1 - core) * CHUNKS)
     for copy in loads[2:4]:
         copy.wait()
-    for b in range(BLOCKS):
-        transposed(wv_ref[b], wvt_ref, b)
-    cur_ref[...] = feat_ref[...].T
-    project(0)
+    high, low = split(feat_ref[...])
+    weights = jnp.concatenate(split(wv_ref[0]), axis=1)
+    both = dot(high, weights)
+    high, low = split(both[:, :CHANNELS] + both[:, CHANNELS:] + dot(low, weights[:, :CHANNELS]))
+    proj_ref[:, :CHANNELS] = high
+    proj_ref[:, CHANNELS:] = low
     for b in range(BLOCKS):
         order = [(1 - core) * CHUNKS + q for q in range(CHUNKS)] + [core * CHUNKS + q for q in range(CHUNKS)]
-        if b == 0:
-            table(order[0])
         for k, chunk in enumerate(order):
             q = k % CHUNKS
             part_ref = away_ref.at[b, q] if k < CHUNKS else home_ref.at[b, q]
-            part_ref[...] = factor(chunk_rows(chunk))
             if b == 0 and k + 1 < len(order):
-                table(order[k + 1])
-            if k < CHUNKS:
-                if comm and b == 0 and q == 0:
+
+                def step(i, _, chunk=chunk, part_ref=part_ref, following=order[k + 1]):
+                    rows = pl.ds(pl.multiple_of(chunk * CHUNK + i * FUSED, FUSED), FUSED)
+                    part = factor(rows)
+                    table_rows(following, i, FUSED)
+                    part_ref[pl.ds(pl.multiple_of(i * FUSED, FUSED), FUSED), :] = part
+                    return 0
+
+                lax.fori_loop(0, CHUNK // FUSED, step, 0)
+            else:
+                part_ref[...] = factor(chunk_rows(chunk))
+            if b:
+                ready = [k]
+            elif k < CHUNKS - 1:
+                ready = []
+            elif k == CHUNKS - 1:
+                if comm:
                     pl.semaphore_wait(barrier, len(PLANE_PEERS) + len(Z_PEERS) + 1)
-                send(part_ref, cross_ref.at[b, q], cross_send.at[b, q], cross_recv.at[b, q], other_core)
+                ready = list(range(CHUNKS))
             else:
-                wait(cross_ref.at[b, q], cross_recv.at[b, q])
-                part_ref[...] += cross_ref[b, q]
-                for delta in PLANE_PEERS:
-                    peer, to = plane_peer(delta)
-                    send(
-                        home_ref.at[b, q, pl.ds(pl.multiple_of(peer * PIECE, 8), PIECE)],
-                        plane_ref.at[b, q, me], plane_send.at[b, q], plane_recv.at[b, q], to,
-                    )
-                plane_ref[b, q, me] = home_ref[b, q, pl.ds(pl.multiple_of(me * PIECE, 8), PIECE)]
+                ready = [k]
+            for j in ready:
+                if j < CHUNKS:
+                    hand_over(b, j)
+                else:
+                    reduce_plane(b, j - CHUNKS)
         if b == 0:
             for copy in loads[4:]:
                 copy.wait()
+            cur_ref[...] = feat_ref[...].T
             for i in range(BLOCKS):
+                if i:
+                    transposed(wv_ref[i], wvt_ref, i)
                 transposed(wh_ref[i] * gain_ref[i : i + 1, :].T, wht_ref, i)
                 transposed(wo_ref[i], wot_ref, i)
                 bht_ref[i] = jnp.broadcast_to(bh_ref[i : i + 1, :], (CHANNELS, CHANNELS)).T

time: 56.5 us -> 55.1 us (0.975)
  Pallas kernels: 55.6 us -> 54.2 us
    pallas_call x1, Pallas kernels: 55.6 us -> 54.2 us  [local(): pl.pallas_call(functools.partial(body, comm=comm), name='ewald', out_shap...]
where the time goes in v3:
time: 55.1 us; the launch traced here: 55 us
  Pallas kernels  54.2 us (98%)
  local copies, waits for them, and re-layouts  0.8 us (1%)
    pallas_call x1, Pallas kernels, local(): pl.pallas_call(functools.partial(body, comm=comm), name='ewald', out_shap...  54.2 us

profile of v3, /device:TPU:1, one launch (start us, length us, event | category | flops | bytes accessed | tf_op | source)
XLA Modules:
  0.0 55.0 jit_solution(13339285835634763846)
XLA Ops:
  0.0 54.2 %ewald.1 = f32[1024,128]{1,0:T(8,128)S(1)} custom-call(f32[1024,128]{1,0:T(8,128)} %feat_hbm.1, s32[3,1024]{1,0:T(4,128)} %pos_hbm.1, s32[3,768]{1,0:T(4,128)} %wave_hbm.1, f32[2,128,128]{2,1,0:T(8,128)} %wv_hbm.1, f32[2,768,128]{2,1,0:T(8,128)} %filt_hbm.1, f32[2,128]{1,0:T(2,128)} %gain_hbm.1, f32[2,128,128]{2,1,0:T(8,128)} %wh_hbm.1, f32[2,128]{1,0:T(2,128)} %bh_hbm.1, ...), custom_call_target="tpu_custom_call" | custom-call | tf_op jit(solution)/shard_map/ewald/pallas_call | solution.py:288
  54.2 0.8 %copy.11 = f32[1024,128]{1,0:T(8,128)} copy(f32[1024,128]{1,0:T(8,128)S(1)} %ewald.1) | data formatting | bytes 1048576

commit v4 on v3

--- a/solution.py
+++ b/solution.py
@@ -21,7 +21,6 @@
 PIECE = CHUNK // PLANE
 TURN = 262144.0
 FUSED = 256
-GROUP = 32
 TAIL = ((0, CHUNKS - 1), (CHUNKS - 1, CHUNKS))
 
 SIN = (4.442882834149947, -7.308241154547219, 3.6062889582380353, -0.8457635962127477, 0.10920575375428615)
@@ -83,21 +82,27 @@
         copy.start()
 
     outer, atoms = lax.axis_index("outer"), lax.axis_index("atoms")
-    core, y = outer % 2, (atoms % 2) * 2 + outer // 2
-    x, z = (atoms // 2) % NX, atoms // (2 * NX)
+    core, y = lax.rem(outer, 2), lax.rem(atoms, 2) * 2 + lax.div(outer, 2)
+    x, z = lax.rem(lax.div(atoms, 2), NX), lax.div(atoms, 2 * NX)
     me = x * NY + y
 
     def device(x, y, z, core):
-        return ((y % 2) * 2 + core, z * (2 * NX) + x * 2 + y // 2)
+        return (lax.rem(y, 2) * 2 + core, z * (2 * NX) + x * 2 + lax.div(y, 2))
+
+    plane_peers, z_peers = {}, {}
+    for delta in PLANE_PEERS:
+        px, py = lax.rem(x + delta[0], NX), lax.rem(y + delta[1], NY)
+        plane_peers[delta] = (px * NY + py, device(px, py, z, core))
+    for delta in Z_PEERS:
+        z_peers[delta] = device(x, y, lax.rem(z + delta, NZ), core)
 
     def plane_peer(delta):
-        px, py = (x + delta[0]) % NX, (y + delta[1]) % NY
-        return px * NY + py, device(px, py, z, core)
+        return plane_peers[delta]
 
     other_core = device(x, y, z, 1 - core)
 
     def z_peer(delta):
-        return device(x, y, (z + delta) % NZ, core)
+        return z_peers[delta]
 
     def send(source, target, send_sem, recv_sem, to):
         if comm:
@@ -151,16 +156,16 @@
         table_rows(chunk, 0, CHUNK)
 
     def table_rows(chunk, i, group):
-            for j in range(group // 16):
-                octet = chunk * (CHUNK // 16) + i * (group // 16) + j
-                t = turn_ref[pl.ds(pl.multiple_of(octet * 8, 8), 8), :]
-                r = t - jnp.round(t)
-                u = r * r
-                s = horner(SIN, u) * r
-                high, low = split(jnp.concatenate([1.0 - s * s, s * horner(COS, u)], axis=0))
-                at = pl.ds(pl.multiple_of(octet * 16, 16), 16)
-                high_ref[at, :] = high
-                low_ref[at, :] = low
+        for j in range(group // 16):
+            octet = chunk * (CHUNK // 16) + i * (group // 16) + j
+            t = turn_ref[pl.ds(pl.multiple_of(octet * 8, 8), 8), :]
+            r = t - jnp.round(t)
+            u = r * r
+            s = horner(SIN, u) * r
+            high, low = split(jnp.concatenate([1.0 - s * s, s * horner(COS, u)], axis=0))
+            at = pl.ds(pl.multiple_of(octet * 16, 16), 16)
+            high_ref[at, :] = high
+            low_ref[at, :] = low
 
     def factor(rows):
         a = dot(high_ref[rows, :], proj_ref[...])

time: 55.1 us -> 55 us (level)
  no operation moved by 1% of the time
where the time goes in v4:
time: 55 us; the launch traced here: 54.8 us
  Pallas kernels  54 us (98%)
  local copies, waits for them, and re-layouts  0.8 us (1%)
    pallas_call x1, Pallas kernels, local(): pl.pallas_call(functools.partial(body, comm=comm), name='ewald', out_shap...  54 us

profile of v4, /device:TPU:1, one launch (start us, length us, event | category | flops | bytes accessed | tf_op | source)
XLA Modules:
  0.0 54.8 jit_solution(16880135530108569759)
XLA Ops:
  0.0 54.0 %ewald.1 = f32[1024,128]{1,0:T(8,128)S(1)} custom-call(f32[1024,128]{1,0:T(8,128)} %feat_hbm.1, s32[3,1024]{1,0:T(4,128)} %pos_hbm.1, s32[3,768]{1,0:T(4,128)} %wave_hbm.1, f32[2,128,128]{2,1,0:T(8,128)} %wv_hbm.1, f32[2,768,128]{2,1,0:T(8,128)} %filt_hbm.1, f32[2,128]{1,0:T(2,128)} %gain_hbm.1, f32[2,128,128]{2,1,0:T(8,128)} %wh_hbm.1, f32[2,128]{1,0:T(2,128)} %bh_hbm.1, ...), custom_call_target="tpu_custom_call" | custom-call | tf_op jit(solution)/shard_map/ewald/pallas_call | solution.py:293
  54.0 0.8 %copy.11 = f32[1024,128]{1,0:T(8,128)} copy(f32[1024,128]{1,0:T(8,128)S(1)} %ewald.1) | data formatting | bytes 1048576

commit v5 on v4

--- a/solution.py
+++ b/solution.py
@@ -136,13 +136,11 @@
 
     def transposed(matrix, held, b):
         high, low = split(matrix.T)
-        held[b, :CHANNELS, :] = high
-        held[b, CHANNELS:, :] = low
+        held[b] = jnp.concatenate([high, high, low], axis=1)
 
     def weighted(held, b, value):
         high, low = split(value)
-        both = dot(held[b], high)
-        return both[:CHANNELS] + both[CHANNELS:] + dot(held[b, :CHANNELS, :], low)
+        return dot(held[b], jnp.concatenate([high, low, high], axis=0))
 
     def project(b):
         high, low = split(weighted(wvt_ref, b, cur_ref[...]).T)
@@ -305,9 +303,9 @@
             pltpu.VMEM((ROWS, ATOMS), bf16),
             pltpu.VMEM((CHANNELS, ATOMS), f32),
             pltpu.VMEM((ATOMS, 2 * CHANNELS), bf16),
-            pltpu.VMEM((BLOCKS, 2 * CHANNELS, CHANNELS), bf16),
-            pltpu.VMEM((BLOCKS, 2 * CHANNELS, CHANNELS), bf16),
-            pltpu.VMEM((BLOCKS, 2 * CHANNELS, CHANNELS), bf16),
+            pltpu.VMEM((BLOCKS, CHANNELS, 3 * CHANNELS), bf16),
+            pltpu.VMEM((BLOCKS, CHANNELS, 3 * CHANNELS), bf16),
+            pltpu.VMEM((BLOCKS, CHANNELS, 3 * CHANNELS), bf16),
             pltpu.VMEM((BLOCKS, CHANNELS, CHANNELS), f32),
             pltpu.VMEM((BLOCKS, CHUNKS, CHUNK, CHANNELS), f32),
             pltpu.VMEM((BLOCKS, CHUNKS, CHUNK, CHANNELS), f32),

time: 55 us -> 54.7 us (level)
  no operation moved by 1% of the time
where the time goes in v5:
time: 54.7 us; the launch traced here: 54.5 us
  Pallas kernels  53.7 us (98%)
  local copies, waits for them, and re-layouts  0.8 us (1%)
    pallas_call x1, Pallas kernels, local(): pl.pallas_call(functools.partial(body, comm=comm), name='ewald', out_shap...  53.7 us

profile of v5, /device:TPU:1, one launch (start us, length us, event | category | flops | bytes accessed | tf_op | source)
XLA Modules:
  0.0 54.5 jit_solution(9015315841333439079)
XLA Ops:
  0.0 53.7 %ewald.1 = f32[1024,128]{1,0:T(8,128)S(1)} custom-call(f32[1024,128]{1,0:T(8,128)} %feat_hbm.1, s32[3,1024]{1,0:T(4,128)} %pos_hbm.1, s32[3,768]{1,0:T(4,128)} %wave_hbm.1, f32[2,128,128]{2,1,0:T(8,128)} %wv_hbm.1, f32[2,768,128]{2,1,0:T(8,128)} %filt_hbm.1, f32[2,128]{1,0:T(2,128)} %gain_hbm.1, f32[2,128,128]{2,1,0:T(8,128)} %wh_hbm.1, f32[2,128]{1,0:T(2,128)} %bh_hbm.1, ...), custom_call_target="tpu_custom_call" | custom-call | tf_op jit(solution)/shard_map/ewald/pallas_call | solution.py:291
  53.7 0.8 %copy.11 = f32[1024,128]{1,0:T(8,128)} copy(f32[1024,128]{1,0:T(8,128)S(1)} %ewald.1) | data formatting | bytes 1048576

commit v6 on v5

--- a/solution.py
+++ b/solution.py
@@ -212,12 +212,12 @@
                 part_ref[...] = factor(chunk_rows(chunk))
             if b:
                 ready = [k]
-            elif k < CHUNKS - 1:
+            elif k < CHUNKS - 2:
                 ready = []
-            elif k == CHUNKS - 1:
+            elif k == CHUNKS - 2:
                 if comm:
                     pl.semaphore_wait(barrier, len(PLANE_PEERS) + len(Z_PEERS) + 1)
-                ready = list(range(CHUNKS))
+                ready = list(range(CHUNKS - 1))
             else:
                 ready = [k]
             for j in ready:

time: 54.7 us -> 54.7 us (level)
  no operation moved by 1% of the time
where the time goes in v6:
time: 54.7 us; the launch traced here: 54.6 us
  Pallas kernels  53.8 us (98%)
  local copies, waits for them, and re-layouts  0.8 us (1%)
    pallas_call x1, Pallas kernels, local(): pl.pallas_call(functools.partial(body, comm=comm), name='ewald', out_shap...  53.8 us

profile of v6, /device:TPU:1, one launch (start us, length us, event | category | flops | bytes accessed | tf_op | source)
XLA Modules:
  0.0 54.6 jit_solution(17436077687220323484)
XLA Ops:
  0.0 53.8 %ewald.1 = f32[1024,128]{1,0:T(8,128)S(1)} custom-call(f32[1024,128]{1,0:T(8,128)} %feat_hbm.1, s32[3,1024]{1,0:T(4,128)} %pos_hbm.1, s32[3,768]{1,0:T(4,128)} %wave_hbm.1, f32[2,128,128]{2,1,0:T(8,128)} %wv_hbm.1, f32[2,768,128]{2,1,0:T(8,128)} %filt_hbm.1, f32[2,128]{1,0:T(2,128)} %gain_hbm.1, f32[2,128,128]{2,1,0:T(8,128)} %wh_hbm.1, f32[2,128]{1,0:T(2,128)} %bh_hbm.1, ...), custom_call_target="tpu_custom_call" | custom-call | tf_op jit(solution)/shard_map/ewald/pallas_call | solution.py:291
  53.8 0.8 %copy.11 = f32[1024,128]{1,0:T(8,128)} copy(f32[1024,128]{1,0:T(8,128)S(1)} %ewald.1) | data formatting | bytes 1048576
